TPU v7x, 256 devices: a whole 4x4x8 slice. The times are simulated.
256 devices in a mesh: frame: 32 (over z_hi, y, x), dp: 8 (over z_lo, core).
Axes of the slice: x: 4, y: 4, z: 8 (z_hi: 2, z_lo: 4; z = z_hi * 4 + z_lo), core: 2. Of those that a mesh axis runs over, the one named last changes fastest.
Arguments:
- queries: bfloat16 [16, 64, 32, 2048], P('dp', 'frame'), may hold values from -90 to 90
- keys_saved: bfloat16 [16, 64, 32, 2048], P('dp', 'frame'), may hold values from -6 to 6
- values_saved: bfloat16 [16, 64, 32, 2048], P('dp', 'frame'), may hold values from -6 to 6
- grad_output: bfloat16 [16, 64, 32, 2048], P('dp', 'frame'), may hold values from -6 to 6
- w_out: bfloat16 [2048, 2048], P('frame'), may hold values from -0.125 to 0.125
Outputs:
- grad_queries: bfloat16 [16, 64, 32, 2048], P('dp', 'frame')
- grad_keys: bfloat16 [16, 64, 32, 2048], P('dp', 'frame')
- grad_values: bfloat16 [16, 64, 32, 2048], P('dp', 'frame')
- grad_w_out: float32 [2048, 2048], P(('frame', 'dp'))
All inputs are finite; a program needn't handle non-finite values.
Results may differ from a plain program's by a relative error of at most 0.015.
Values may be sent and summed in bfloat16 or wider, within the bound.
A program may use at most 128 MiB of HBM per device.

v0:
```python
import jax
import jax.numpy as jnp
from jax import lax
from jax.sharding import PartitionSpec as P

HEADS = 16


def on_device(queries, keys_saved, values_saved, grad_output, w_out):
    model_width = w_out.shape[1]
    head_count = HEADS
    head_size = model_width // head_count
    score_scale = head_size ** (-0.5)
    query_p, key_p, value_p, grad_p = (
        lax.all_to_all(queries, "frame", split_axis=2, concat_axis=1, tiled=True),
        lax.all_to_all(keys_saved, "frame", split_axis=2, concat_axis=1, tiled=True),
        lax.all_to_all(values_saved, "frame", split_axis=2, concat_axis=1, tiled=True),
        lax.all_to_all(grad_output, "frame", split_axis=2, concat_axis=1, tiled=True),
    )
    clips_here, frame_count, patch_count, _ = query_p.shape
    shape_heads = (clips_here, frame_count, patch_count, head_count, head_size)
    token_count = clips_here * frame_count * patch_count
    query_h = query_p.reshape(shape_heads)
    key_h = key_p.reshape(shape_heads)
    value_h = value_p.reshape(shape_heads)
    scores = (
        jnp.einsum("bfphd,bgphd->bphfg", query_h, key_h, preferred_element_type=jnp.float32)
        * score_scale
    )
    probs = jax.nn.softmax(scores, axis=-1)
    probs_low = probs.astype(jnp.bfloat16)
    attended = jnp.einsum(
        "bphfg,bgphd->bfphd", probs_low, value_h, preferred_element_type=jnp.float32
    )
    attended = attended.astype(jnp.bfloat16).reshape(token_count, model_width)
    grad_flat = grad_p.reshape(token_count, model_width)
    grad_att = lax.dot_general(
        grad_flat,
        lax.all_gather(w_out, "frame", axis=0, tiled=True),
        (((1,), (1,)), ((), ())),
        preferred_element_type=jnp.float32,
    ).astype(jnp.bfloat16)
    grad_att_h = grad_att.reshape(shape_heads)
    grad_probs = jnp.einsum(
        "bfphd,bgphd->bphfg", grad_att_h, value_h, preferred_element_type=jnp.float32
    )
    row_delta = jnp.sum(probs * grad_probs, axis=-1, keepdims=True)
    grad_scores = (probs * (grad_probs - row_delta)).astype(jnp.bfloat16)
    grad_q = (
        jnp.einsum("bphfg,bgphd->bfphd", grad_scores, key_h, preferred_element_type=jnp.float32)
        * score_scale
    ).astype(jnp.bfloat16)
    grad_k = (
        jnp.einsum("bphfg,bfphd->bgphd", grad_scores, query_h, preferred_element_type=jnp.float32)
        * score_scale
    ).astype(jnp.bfloat16)
    grad_v = jnp.einsum(
        "bphfg,bfphd->bgphd", probs_low, grad_att_h, preferred_element_type=jnp.float32
    ).astype(jnp.bfloat16)
    layout = (clips_here, frame_count, patch_count, model_width)
    grad_q, grad_k, grad_v = (
        lax.all_to_all(grad_q.reshape(layout), "frame", split_axis=1, concat_axis=2, tiled=True),
        lax.all_to_all(grad_k.reshape(layout), "frame", split_axis=1, concat_axis=2, tiled=True),
        lax.all_to_all(grad_v.reshape(layout), "frame", split_axis=1, concat_axis=2, tiled=True),
    )
    attended_t = attended.T
    grad_weight = lax.psum_scatter(
        jnp.dot(attended_t, grad_flat, preferred_element_type=jnp.float32),
        ("frame", "dp"),
        scatter_dimension=0,
        tiled=True,
    )
    return (grad_q, grad_k, grad_v, grad_weight)


def solution(mesh):
    placed = (
        P("dp", "frame", None, None),
        P("dp", "frame", None, None),
        P("dp", "frame", None, None),
        P("dp", "frame", None, None),
        P("frame", None),
    )
    return jax.shard_map(
        on_device,
        mesh=mesh,
        in_specs=placed,
        out_specs=(
            P("dp", "frame", None, None),
            P("dp", "frame", None, None),
            P("dp", "frame", None, None),
            P(("frame", "dp"), None),
        ),
        check_vma=False,
    )
```

profile of v0, /device:TPU:1, one launch (start us, length us, event | category | flops | bytes accessed | tf_op | source)
XLA Modules:
  0.0 1469.1 jit_solution(10286893894771496737)
XLA Ops:
  8.0 0.7 all-gather.2.cloned.1.call-update
  8.7 2.4 copy.37
  11.1 14.5 all-to-all-start
  25.6 2.4 copy.39
  28.0 11.4 all-to-all-done
  39.4 4.8 all-to-all-start.1
  44.2 2.4 copy.45
  46.6 10.7 all-to-all-done.1
  57.2 3.9 all-to-all-start.3
  61.1 2.4 copy.43
  63.5 20.6 %all-to-all-done.3 = bf16[2,2,32,2048]{3,1,0,2:T(2,128)(2,1)S(1)} async-done(((bf16[2,2,32,2048]{3,1,0,2:T(2,128)(2,1)}), bf16[2,2,32,2048]{3,1,0,2:T(2,128)(2,1)S(1)}, u32[]{:S(2)}, u32[]{:S(2)}) %all-to-all-start.3) | async-done | bytes 524320 | tf_op jit(solution)/shard_map/all_to_all | solution.py:17
  84.2 9.9 all-to-all-start.2
  94.3 0.4 copy.38
  94.7 0.3 reshape.101
  95.0 0.4 copy.40
  95.4 0.3 reshape.102
  95.7 0.4 copy.46
  96.1 0.3 reshape.105
  96.5 10.6 all-to-all-done.2
  107.0 0.4 copy.44
  107.6 0.6 fusion.34
  108.1 0.4 fusion.8
  108.5 0.3 copy.61
  108.9 8.1 fusion.10
  117.0 74.6 %all-gather.2.cloned.1.call-done = bf16[2048,2048]{1,0:T(8,128)(2,1)} async-done(((bf16[64,2048]{1,0:T(8,128)(2,1)}), bf16[2048,2048]{1,0:T(8,128)(2,1)}) %all-gather.2.cloned.1.call-update) | async-done | bytes 8388624 | tf_op jit(solution)/shard_map/all_gather | solution.py:39
  191.6 6.3 fusion.7
  198.1 0.8 copy-done
  198.9 0.3 fusion.9
  199.2 0.3 copy.69
  199.5 0.9 reshape.112
  200.4 4.6 all-to-all-start.6
  205.0 1.5 multiply_reduce_fusion
  206.5 0.3 multiply_convert_fusion
  206.8 0.3 fusion.5
  207.1 0.3 copy.68
  207.5 0.9 reshape.111
  208.4 12.5 all-to-all-done.6
  220.9 4.3 all-to-all-start.5
  225.2 0.3 fusion.6
  225.5 0.3 copy.67
  225.9 0.9 reshape.110
  226.8 12.4 all-to-all-done.5
  239.2 3.9 all-to-all-start.4
  243.1 1.1 copy.64
  244.2 1.1 copy.63
  245.3 11.1 all-to-all-done.4
  256.3 1.1 copy.62
  257.4 1204.3 %reduce-scatter.2.cloned.1.call-done = f32[8,2048]{1,0:T(8,128)} async-done(((f32[2048,2048]{1,0:T(8,128)}), f32[8,2048]{1,0:T(8,128)}) %reduce-scatter.2.cloned.1.call-update) | async-done | bytes 65552 | tf_op jit(solution)/shard_map/reduce_scatter | solution.py:67
  (6 shorter events, 0.6 us)
Async XLA Ops:
  8.0 183.6 %all-gather.2.cloned.1.call-start = ((), (), s32[]{:S(2)}) async-start(), calls=%async_computation.8 | async-start | bytes 8650752 | tf_op jit(solution)/shard_map/all_gather | solution.py:39
  11.1 28.3 %all-to-all-start = ((bf16[2,2,32,2048]{3,1,0,2:T(2,128)(2,1)}), bf16[2,2,32,2048]{3,1,0,2:T(2,128)(2,1)S(1)}, u32[]{:S(2)}, u32[]{:S(2)}) async-start(bf16[2,2,32,2048]{3,1,0,2:T(2,128)(2,1)} %copy.37), calls=%async_computation | async-start | bytes 1048576 | tf_op jit(solution)/shard_map/all_to_all | solution.py:15
  39.4 17.8 %all-to-all-start.1 = ((bf16[2,2,32,2048]{3,1,0,2:T(2,128)(2,1)}), bf16[2,2,32,2048]{3,1,0,2:T(2,128)(2,1)S(1)}, u32[]{:S(2)}, u32[]{:S(2)}) async-start(bf16[2,2,32,2048]{3,1,0,2:T(2,128)(2,1)} %copy.39), calls=%async_computation.1 | async-start | bytes 1048576 | tf_op jit(solution)/shard_map/all_to_all | solution.py:16
  57.2 26.9 %all-to-all-start.3 = ((bf16[2,2,32,2048]{3,1,0,2:T(2,128)(2,1)}), bf16[2,2,32,2048]{3,1,0,2:T(2,128)(2,1)S(1)}, u32[]{:S(2)}, u32[]{:S(2)}) async-start(bf16[2,2,32,2048]{3,1,0,2:T(2,128)(2,1)} %copy.45), calls=%async_computation.3 | async-start | bytes 1048576 | tf_op jit(solution)/shard_map/all_to_all | solution.py:17
  84.2 22.9 %all-to-all-start.2 = ((bf16[2,2,32,2048]{3,1,0,2:T(2,128)(2,1)}), bf16[2,2,32,2048]{3,1,0,2:T(2,128)(2,1)S(1)}, u32[]{:S(2)}, u32[]{:S(2)}) async-start(bf16[2,2,32,2048]{3,1,0,2:T(2,128)(2,1)} %copy.43), calls=%async_computation.2 | async-start | bytes 1048576 | tf_op jit(solution)/shard_map/all_to_all | solution.py:18
  94.1 1367.6 %reduce-scatter.2.cloned.1.call-start = ((), (), s32[]{:S(2)}) async-start(), calls=%async_computation.9 | async-start | bytes 16842752 | tf_op jit(solution)/shard_map/reduce_scatter | solution.py:67
  198.1 0.8 copy-start
  200.4 20.5 %all-to-all-start.6 = ((bf16[2,64,1,2048]{3,0,2,1:T(2,128)(2,1)}), bf16[2,64,1,2048]{3,0,2,1:T(2,128)(2,1)S(1)}, u32[]{:S(2)}, u32[]{:S(2)}) async-start(bf16[2,64,1,2048]{3,0,2,1:T(2,128)(2,1)} %reshape.112), calls=%async_computation.6 | async-start | bytes 1048576 | tf_op jit(solution)/shard_map/all_to_all | solution.py:64
  220.9 18.3 %all-to-all-start.5 = ((bf16[2,64,1,2048]{3,0,2,1:T(2,128)(2,1)}), bf16[2,64,1,2048]{3,0,2,1:T(2,128)(2,1)S(1)}, u32[]{:S(2)}, u32[]{:S(2)}) async-start(bf16[2,64,1,2048]{3,0,2,1:T(2,128)(2,1)} %reshape.111), calls=%async_computation.5 | async-start | bytes 1048576 | tf_op jit(solution)/shard_map/all_to_all | solution.py:63
  239.2 17.1 %all-to-all-start.4 = ((bf16[2,64,1,2048]{3,0,2,1:T(2,128)(2,1)}), bf16[2,64,1,2048]{3,0,2,1:T(2,128)(2,1)S(1)}, u32[]{:S(2)}, u32[]{:S(2)}) async-start(bf16[2,64,1,2048]{3,0,2,1:T(2,128)(2,1)} %reshape.110), calls=%async_computation.4 | async-start | bytes 1048576 | tf_op jit(solution)/shard_map/all_to_all | solution.py:62
Sparse Core Ops, SparseCore 0:
  12.4 179.2 all-gather.1
Sparse Core Ops, SparseCore 1:
  117.1 1344.6 reduce-scatter.1
where the time goes:
time: 1470 us
  waiting for transfers between devices  1370 us (93%)
  starting transfers between devices  46.1 us (3%)
  local copies, waits for them, and re-layouts  20.5 us (1%)
  matrix products  17.7 us (1%)
  between operations  15.7 us (1%)
    reduce_scatter x1, waiting for transfers between devices, on_device(): lax.psum_scatter(jnp.dot(attended_t, grad_flat, preferred_element_type=jn...  1200 us
    all_gather x1, waiting for transfers between devices, on_device(): lax.all_gather(w_out, 'frame', axis=0, tiled=True)  74.6 us
  transfers between devices with their start and end apart: 9, of which 9 were waited for; matrix products, arithmetic and copies ran while one was open for 3% of the time, Pallas kernels for 0%

commit v1 on v0

v1 whole, which is shorter than its diff:
```python
import functools

import jax
import jax.numpy as jnp
from jax import lax
from jax.experimental import pallas as pl
from jax.experimental.pallas import tpu as pltpu
from jax.sharding import PartitionSpec as P

F32 = jnp.float32
BF16 = jnp.bfloat16
D = 2048
HEAD_DIM = 128
SCALE = HEAD_DIM ** (-0.5)
Q, K, V, G = 0, 1, 2, 3
NT = (((1,), (1,)), ((), ()))
NN = (((1,), (0,)), ((), ()))
TN = (((0,), (0,)), ((), ()))


def dot(a, b, dims):
    return lax.dot_general(a, b, dims, preferred_element_type=F32)


def coords():
    f = lax.axis_index("frame")
    d = lax.axis_index("dp")
    return f // 16, (f // 4) % 4, f % 4, d // 2, d % 2


def dev(zh, y, x, zl, core):
    return {"frame": zh * 16 + y * 4 + x, "dp": zl * 2 + core}


def kernel(
    q_ref, k_ref, v_ref, g_ref, w_ref,
    oq_ref, ok_ref, ov_ref, ow_ref,
    zin, xs, xg, rx, rg, wg, att, gat, os, ro, zs, g1s, g1r, g2s, g2r, g3s, g3r,
    sA, rA, sW, rW, sB, rB, sR, rR, sD, rD, sG, rG,
):
    zh, y, x, zl, core = coords()
    me = y * 4 + x
    ins = (q_ref, k_ref, v_ref, g_ref)
    outs = (oq_ref, ok_ref, ov_ref)
    mine = pl.ds(pl.multiple_of(zh * 16, 16), 16)
    other = pl.ds(pl.multiple_of((1 - zh) * 16, 16), 16)
    pair = dev(1 - zh, y, x, zl, core)
    sibling = dev(zh, y, x, zl, 1 - core)

    def plane(t):
        return lax.rem(y + t // 4, 4), lax.rem(x + lax.rem(t, 4), 4)

    def zdev(t):
        z = lax.rem(zh * 4 + zl + t, 8)
        return z, dev(z // 4, y, x, lax.rem(z, 4), core)

    def send(src, dst, s, r, to):
        cp = pltpu.make_async_remote_copy(
            src_ref=src, dst_ref=dst, send_sem=s, recv_sem=r, device_id=to
        )
        cp.start()

    def drain(ref, sem):
        pltpu.make_async_copy(ref, ref, sem).wait()

    barrier = pltpu.get_barrier_semaphore()

    @pl.loop(1, 16)
    def _(t):
        ty, tx = plane(t)
        pl.semaphore_signal(barrier, inc=1, device_id=dev(zh, ty, tx, zl, core))

    @pl.loop(1, 8)
    def _(t):
        _, to = zdev(t)
        pl.semaphore_signal(barrier, inc=1, device_id=to)

    pl.semaphore_signal(barrier, inc=1, device_id=sibling)
    pl.semaphore_wait(barrier, 23)

    half = pl.ds(pl.multiple_of(core * 32, 32), 32)
    send(w_ref.at[half], wg.at[zh, x, core], sW.at[0], rW.at[0], pair)
    order = (G, Q, K, V)
    for c in range(2):
        for a in order:
            send(ins[a].at[c, :, other], zin.at[a, c], sA.at[a, c], rA.at[a, c], pair)
    wg[zh, x, core] = w_ref[half]

    def source(r):
        return lax.rem(r // 8, 2) * 32 + lax.rem(r // 4, 2) * 16 + (r // 16) * 4 + lax.rem(r, 4)

    rows = lax.broadcasted_iota(jnp.int32, (64, 64), 0)
    cols = lax.broadcasted_iota(jnp.int32, (64, 64), 1)
    perm = jnp.where(source(rows) == cols, 1.0, 0.0).astype(BF16)
    unperm = jnp.where(source(cols) == rows, 1.0, 0.0).astype(BF16)

    def spread(a, c):
        drain(zin.at[a, c], rA.at[a, c])
        own = ins[a][c, :, mine, :].reshape(32, D)
        far = zin[a, c].reshape(32, D)
        out = dot(perm, jnp.concatenate([own, far], axis=0), NN).astype(BF16)
        if a == G:
            xg[c] = out.reshape(4, 16, D)
            rg[c, me] = xg[c, x]

            @pl.loop(1, 16)
            def _(t):
                ty, tx = plane(t)
                send(xg.at[c, tx], rg.at[c, me], sB.at[a, c], rB.at[a, c], dev(zh, ty, tx, zl, core))
        else:
            for i in range(4):
                for j in range(4):
                    part = out[i * 16:i * 16 + 16]
                    xs[a, c, i * 4 + j] = jnp.concatenate(
                        [part[:, j * 256:j * 256 + 256], part[:, 1024 + j * 256:1280 + j * 256]], axis=1
                    )
            rx[a, c, me] = xs[a, c, x * 4 + y]

            @pl.loop(1, 16)
            def _(t):
                ty, tx = plane(t)
                send(xs.at[a, c, tx * 4 + ty], rx.at[a, c, me], sB.at[a, c], rB.at[a, c], dev(zh, ty, tx, zl, core))

    def w_second():
        drain(wg.at[0, 0, 0], rW.at[0])

        @pl.loop(1, 4)
        def _(t):
            send(wg.at[:, x, core], wg.at[:, x, core], sW.at[1], rW.at[1], dev(zh, y, lax.rem(x + t, 4), zl, core))

    def w_third():
        drain(wg.at[:, pl.ds(0, 3), 0], rW.at[1])
        send(wg.at[:, :, core], wg.at[:, :, core], sW.at[2], rW.at[2], sibling)

    lane = lax.broadcasted_iota(jnp.int32, (256, 256), 1)
    line = lax.broadcasted_iota(jnp.int32, (256, 256), 0)
    same = lax.rem(lane, 4) == lax.rem(line, 4)

    def attend(c):
        drain(rg.at[c, pl.ds(0, 15)], rB.at[G, c])
        go = rg[c].reshape(256, D)
        for h in range(2):
            gat[:, h * 256:h * 256 + 256] = dot(go, wg[h].reshape(256, D), NT).astype(BF16)
        for a in (Q, K, V):
            drain(rx.at[a, c, pl.ds(0, 15)], rB.at[a, c])

        @pl.loop(0, 4)
        def _(h):
            col = pl.ds(pl.multiple_of(h * HEAD_DIM, HEAD_DIM), HEAD_DIM)
            query = rx[Q, c, :, :, col].reshape(256, HEAD_DIM)
            key = rx[K, c, :, :, col].reshape(256, HEAD_DIM)
            value = rx[V, c, :, :, col].reshape(256, HEAD_DIM)
            ga = gat[:, col]
            scores = jnp.where(same, dot(query, key, NT) * SCALE, -1e30)
            e = jnp.exp(scores - jnp.max(scores, axis=1, keepdims=True))
            probs = e * (1.0 / jnp.sum(e, axis=1, keepdims=True))
            low = probs.astype(BF16)
            att[c, :, col] = dot(low, value, NN).astype(BF16)
            gp = dot(ga, value, NT)
            delta = jnp.sum(probs * gp, axis=1, keepdims=True)
            gs = (probs * (gp - delta)).astype(BF16)
            os[Q, c, :, :, col] = (dot(gs, key, NN) * SCALE).astype(BF16).reshape(16, 16, HEAD_DIM)
            os[K, c, :, :, col] = (dot(gs, query, TN) * SCALE).astype(BF16).reshape(16, 16, HEAD_DIM)
            os[V, c, :, :, col] = dot(low, ga, TN).astype(BF16).reshape(16, 16, HEAD_DIM)

        slot = x * 4 + y
        for a in range(3):
            ro[a, c, slot] = os[a, c, me]

            @pl.loop(1, 16)
            def _(t):
                ty, tx = plane(t)
                send(os.at[a, c, ty * 4 + tx], ro.at[a, c, slot], sR.at[a, c], rR.at[a, c], dev(zh, ty, tx, zl, core))

    def give_back(a, c):
        drain(ro.at[a, c, pl.ds(0, 15)], rR.at[a, c])
        parts = []
        for i in range(4):
            row = [ro[a, c, i * 4 + j] for j in range(4)]
            parts.append(
                jnp.concatenate([r[:, :256] for r in row] + [r[:, 256:] for r in row], axis=1)
            )
        out = dot(unperm, jnp.concatenate(parts, axis=0), NN).astype(BF16)
        zs[a, c] = out[32:].reshape(2, 16, D)
        send(zs.at[a, c], outs[a].at[c, :, mine], sD.at[a, c], rD.at[a, c], pair)
        outs[a][c, :, mine, :] = out[:32].reshape(2, 16, D)

    def weight_first():
        @pl.loop(0, 8)
        def _(n):
            col = pl.ds(pl.multiple_of(n * 256, 256), 256)
            go = rg[:, :, :, col].reshape(512, 256)
            part = dot(att[...].reshape(512, 512), go, TN)
            part = part.reshape(8, 4, 2, 8, 256)
            for i in range(2):
                g1s[i, :, :, :, col] = part[:, :, i].reshape(2, 4, 32, 256).astype(BF16)

        send(g1s.at[1 - core], g1r, sG.at[0], rG.at[0], sibling)

    def weight_second():
        drain(g1r, rG.at[0])
        for i in range(4):
            g2s[i] = (g1s[core, :, i].astype(F32) + g1r[:, i].astype(F32)).astype(BF16)
        g2r[x] = g2s[x]

        @pl.loop(1, 4)
        def _(t):
            tx = lax.rem(x + t, 4)
            send(g2s.at[tx], g2r.at[x], sG.at[1], rG.at[1], dev(zh, y, tx, zl, core))

    def weight_third():
        drain(g2r.at[pl.ds(0, 3)], rG.at[1])
        total = (g2r[0].astype(F32) + g2r[1].astype(F32)) + (g2r[2].astype(F32) + g2r[3].astype(F32))
        total = total.reshape(8, 8, D)
        g3s[...] = jnp.concatenate([total[:, :, :1024], total[:, :, 1024:]], axis=1).astype(BF16)
        z0, _ = zdev(0)
        g3r[z0] = g3s[z0]

        @pl.loop(1, 8)
        def _(t):
            z, to = zdev(t)
            send(g3s.at[z], g3r.at[z0], sG.at[2], rG.at[2], to)

    def weight_last():
        drain(g3r.at[pl.ds(0, 7)], rG.at[2])
        total = g3r[0].astype(F32)
        for i in range(1, 8):
            total = total + g3r[i].astype(F32)
        ow_ref[:, :1024] = total[:8]
        ow_ref[:, 1024:] = total[8:]

    w_second()
    spread(G, 0)
    w_third()
    for a in (Q, K, V):
        spread(a, 0)
    drain(wg.at[:, :, 0], rW.at[2])
    attend(0)
    spread(G, 1)
    for a in range(3):
        give_back(a, 0)
    for a in (Q, K, V):
        spread(a, 1)
    attend(1)
    weight_first()
    for a in range(3):
        give_back(a, 1)
    weight_second()
    weight_third()
    weight_last()

    drain(wg.at[0, 0, 0], sW.at[0])
    drain(wg.at[:, pl.ds(0, 3), 0], sW.at[1])
    drain(wg.at[:, :, 0], sW.at[2])
    for c in range(2):
        for a in (Q, K, V, G):
            drain(zin.at[a, c], sA.at[a, c])
        drain(rg.at[c, pl.ds(0, 15)], sB.at[G, c])
        for a in (Q, K, V):
            drain(rx.at[a, c, pl.ds(0, 15)], sB.at[a, c])
            drain(ro.at[a, c, pl.ds(0, 15)], sR.at[a, c])
            drain(zs.at[a, c], sD.at[a, c])
            drain(zs.at[a, c], rD.at[a, c])
    drain(g1r, sG.at[0])
    drain(g2r.at[pl.ds(0, 3)], sG.at[1])
    drain(g3r.at[pl.ds(0, 7)], sG.at[2])


def on_device(queries, keys_saved, values_saved, grad_output, w_out):
    vmem = pl.BlockSpec(memory_space=pltpu.VMEM)
    dma = pltpu.SemaphoreType.DMA
    whole = jax.ShapeDtypeStruct(queries.shape, BF16)
    return pl.pallas_call(
        kernel,
        name="attention_backward",
        out_shape=(whole, whole, whole, jax.ShapeDtypeStruct((8, D), F32)),
        in_specs=[vmem] * 5,
        out_specs=(vmem,) * 4,
        scratch_shapes=[
            pltpu.VMEM((4, 2, 2, 16, D), BF16),
            pltpu.VMEM((3, 2, 16, 16, 512), BF16),
            pltpu.VMEM((2, 4, 16, D), BF16),
            pltpu.VMEM((3, 2, 16, 16, 512), BF16),
            pltpu.VMEM((2, 16, 16, D), BF16),
            pltpu.VMEM((2, 4, 2, 32, D), BF16),
            pltpu.VMEM((2, 256, 512), BF16),
            pltpu.VMEM((256, 512), BF16),
            pltpu.VMEM((3, 2, 16, 16, 512), BF16),
            pltpu.VMEM((3, 2, 16, 16, 512), BF16),
            pltpu.VMEM((3, 2, 2, 16, D), BF16),
            pltpu.VMEM((2, 2, 4, 32, D), BF16),
            pltpu.VMEM((2, 4, 32, D), BF16),
            pltpu.VMEM((4, 2, 32, D), BF16),
            pltpu.VMEM((4, 2, 32, D), BF16),
            pltpu.VMEM((8, 16, 1024), BF16),
            pltpu.VMEM((8, 16, 1024), BF16),
            dma((4, 2)), dma((4, 2)),
            dma((3,)), dma((3,)),
            dma((4, 2)), dma((4, 2)),
            dma((3, 2)), dma((3, 2)),
            dma((3, 2)), dma((3, 2)),
            dma((3,)), dma((3,)),
        ],
        compiler_params=pltpu.CompilerParams(
            collective_id=0, has_side_effects=True, vmem_limit_bytes=56 * 1024 * 1024
        ),
        cost_estimate=pl.CostEstimate(flops=5 * 10**9, bytes_accessed=4 * 2**20, transcendentals=2**20),
    )(queries, keys_saved, values_saved, grad_output, w_out)


def solution(mesh):
    split = P("dp", "frame", None, None)
    return jax.shard_map(
        on_device,
        mesh=mesh,
        in_specs=(split, split, split, split, P("frame", None)),
        out_specs=(split, split, split, P(("frame", "dp"), None)),
        check_vma=False,
    )
```

time: 1470 us -> 132 us (0.09)
  waiting for transfers between devices: 1370 us -> 0 us
  Pallas kernels: 0 us -> 126 us
  starting transfers between devices: 46.1 us -> 0 us
  matrix products: 17.7 us -> 0 us
  local copies, waits for them, and re-layouts: 20.5 us -> 4.66 us
  between operations: 15.7 us -> 0.65 us
    reduce_scatter x1 -> x0, waiting for transfers between devices: 1200 us -> none  [on_device(): lax.psum_scatter(jnp.dot(attended_t, grad_flat, preferred_element_type=jn...]
    pallas_call x0 -> x1, Pallas kernels: none -> 126 us  [on_device(): pl.pallas_call(kernel, name='attention_backward', out_shape=(whole, whole...]
    all_to_all x7 -> x0, waiting for transfers between devices: 89.2 us -> none  [the longest x1 20.6 us: on_device(): lax.all_to_all(values_saved, 'frame', split_axis=2, concat_axis=1, tiled=...]
    all_gather x1 -> x0, waiting for transfers between devices: 74.6 us -> none  [on_device(): lax.all_gather(w_out, 'frame', axis=0, tiled=True)]
    all_to_all x7 -> x0, starting transfers between devices: 45.9 us -> none  [the longest x1 14.5 us: on_device(): lax.all_to_all(queries, 'frame', split_axis=2, concat_axis=1, tiled=True)]
    dot_general x7 -> x0, matrix products: 17.2 us -> none  [the longest x1 8.12 us: on_device(): jnp.dot(attended_t, grad_flat, preferred_element_type=jnp.float32)]
  transfers between devices with their start and end apart: 9 -> 0, of which waited for: 9 -> 0; matrix products, arithmetic and copies ran while one was open for 3% -> 0% of each run, Pallas kernels for 0% -> 0%
where the time goes in v1:
time: 132 us; the launch traced here: 131 us
  Pallas kernels  126 us (95%)
  local copies, waits for them, and re-layouts  4.66 us (4%)
    pallas_call x1, Pallas kernels, on_device(): pl.pallas_call(kernel, name='attention_backward', out_shape=(whole, whole...  126 us
    unnamed x10, local copies, waits for them, and re-layouts  4.66 us

profile of v1, /device:TPU:1, one launch (start us, length us, event | category | flops | bytes accessed | tf_op | source)
XLA Modules:
  0.0 131.0 jit_solution(10445877339434788810)
XLA Ops:
  0.6 125.7 %attention_backward.1 = (bf16[2,2,32,2048]{3,2,1,0:T(8,128)(2,1)}, bf16[2,2,32,2048]{3,2,1,0:T(8,128)(2,1)}, bf16[2,2,32,2048]{3,2,1,0:T(8,128)(2,1)}, f32[8,2048]{1,0:T(8,128)}) custom-call(bf16[2,2,32,2048]{3,2,1,0:T(8,128)(2,1)} %q_ref.1, bf16[2,2,32,2048]{3,2,1,0:T(8,128)(2,1)} %k_ref.1, bf16[2,2,32,2048]{3,2,1,0:T(8,128)(2,1)} %v_ref.1, ...), custom_call_target="tpu_custom_call" | custom-call | flops 5000000000 | bytes 4194304 | tf_op jit(solution)/shard_map/attention_backward/pallas_call | solution.py:273
  126.3 0.0 copy-start.1
  126.3 1.9 %copy.13 = bf16[2,2,32,2048]{3,2,1,0:T(8,128)(2,1)} copy(bf16[2,2,32,2048]{3,2,1,0:T(8,128)(2,1)} %get-tuple-element.8) | data formatting | bytes 1048576
  128.3 0.0 copy-done.1
  128.3 0.0 copy-start
  128.3 0.8 copy.14
  129.1 0.4 copy-done
  129.5 0.0 copy-start.2
  129.5 0.8 copy.15
  130.3 0.1 copy-done.2
  130.4 0.6 copy.16
Async XLA Ops:
  126.3 2.0 %copy-start.1 = (bf16[2,2,32,2048]{3,2,1,0:T(8,128)(2,1)S(1)}, bf16[2,2,32,2048]{3,2,1,0:T(8,128)(2,1)}, u32[]{:S(2)}) copy-start(bf16[2,2,32,2048]{3,2,1,0:T(8,128)(2,1)} %get-tuple-element.9) | copy-start | bytes 1572868
  128.3 1.2 copy-start
  129.5 0.9 copy-start.2

commit v2 on v0

v2 whole, which is shorter than its diff:
```python
import jax
import jax.numpy as jnp
from jax import lax
from jax.experimental import pallas as pl
from jax.experimental.pallas import tpu as pltpu
from jax.sharding import PartitionSpec as P

F32 = jnp.float32
BF16 = jnp.bfloat16
D = 2048
HALF = 1024
HEAD_DIM = 128
SCALE = HEAD_DIM ** (-0.5)
Q, K, V, G = 0, 1, 2, 3
NT = (((1,), (1,)), ((), ()))
NN = (((1,), (0,)), ((), ()))
TN = (((0,), (0,)), ((), ()))
DEPTH = 6


def dot(a, b, dims):
    return lax.dot_general(a, b, dims, preferred_element_type=F32)


def coords():
    f = lax.axis_index("frame")
    d = lax.axis_index("dp")
    return f // 16, (f // 4) % 4, f % 4, d // 2, d % 2


def dev(zh, y, x, zl, core):
    return {"frame": zh * 16 + y * 4 + x, "dp": zl * 2 + core}


def kernel(
    q_hbm, k_hbm, v_hbm, g_hbm, w_hbm,
    oq_ref, ok_ref, ov_ref, ow_ref,
    q_ref, k_ref, v_ref, g_ref, w_ref,
    gin, zin, xg, xqk, xv, rg, rqk, rv, wg, att, att_t, os, ro, zs, g1s, g1r, g2s, g2r, g3s, g3r,
    ssem, rsem, lsem,
):
    zh, y, x, zl, core = coords()
    me = y * 4 + x
    ins = (q_ref, k_ref, v_ref, g_ref)
    outs = (oq_ref, ok_ref, ov_ref)
    mine = pl.ds(pl.multiple_of(zh * 16, 16), 16)
    other = pl.ds(pl.multiple_of((1 - zh) * 16, 16), 16)
    halves = (zh, 1 - zh)

    def cols(h):
        return pl.ds(pl.multiple_of(h * HALF, HALF), HALF)

    pair = dev(1 - zh, y, x, zl, core)
    sibling = dev(zh, y, x, zl, 1 - core)

    def plane(t):
        return lax.rem(y + t // 4, 4), lax.rem(x + lax.rem(t, 4), 4)

    numbers = {}
    flight = {}

    def expect(ref, *key):
        numbers[key] = len(numbers)
        flight["s", key] = ref
        flight["r", key] = ref

    def send(src, dst, to, *key):
        n = numbers[key]
        pltpu.make_async_remote_copy(
            src_ref=src, dst_ref=dst, send_sem=ssem.at[n], recv_sem=rsem.at[n], device_id=to
        ).start()

    def drain(way, *key):
        ref = flight.pop((way, key), None)
        if ref is not None:
            sem = (ssem if way == "s" else rsem).at[numbers[key]]
            pltpu.make_async_copy(ref, ref, sem).wait()

    loads = [
        pltpu.make_async_copy(src, dst, lsem.at[i])
        for i, (src, dst) in enumerate(
            zip((q_hbm, k_hbm, v_hbm, g_hbm, w_hbm), (q_ref, k_ref, v_ref, g_ref, w_ref))
        )
    ]
    for load in loads:
        load.start()

    barrier = pltpu.get_barrier_semaphore()

    @pl.loop(1, 16)
    def _(t):
        ty, tx = plane(t)
        pl.semaphore_signal(barrier, inc=1, device_id=dev(zh, ty, tx, zl, core))

    @pl.loop(1, 8)
    def _(t):
        z = lax.rem(zh * 4 + zl + t, 8)
        pl.semaphore_signal(barrier, inc=1, device_id=dev(z // 4, y, x, lax.rem(z, 4), core))

    pl.semaphore_signal(barrier, inc=1, device_id=sibling)
    pl.semaphore_wait(barrier, 23)
    for load in loads:
        load.wait()

    rows_half = pl.ds(pl.multiple_of(core * 32, 32), 32)
    steps = ((0, 0), (0, 1), (1, 0), (1, 1))
    queue = []
    for c, s in steps:
        if s == 0:
            queue.append((G, c, s))
        queue += [(a, c, s) for a in (Q, K, V)]
        if (c, s) == (0, 0):
            queue.append(None)

    def pump(n=1):
        for item in queue[:n]:
            if item is None:
                expect(wg.at[0, 0, 0], "W", 0)
                send(w_ref.at[rows_half], wg.at[zh, x, core], pair, "W", 0)
            elif item[0] == G:
                c = item[1]
                expect(gin.at[c], "A", *item)
                send(g_ref.at[c, :, other], gin.at[c], pair, "A", *item)
            else:
                a, c, s = item
                expect(zin.at[a, c, s], "A", *item)
                send(ins[a].at[c, :, other, cols(halves[1 - s])], zin.at[a, c, s], pair, "A", *item)
        del queue[:n]

    pump(DEPTH)

    def w_along(s):
        if s == 1:
            drain("r", "W", 0)
            pump()
        h = halves[s]
        expect(wg.at[0, pl.ds(0, 3), 0], "X", s)

        @pl.loop(1, 4)
        def _(t):
            send(wg.at[h, x, core], wg.at[h, x, core], dev(zh, y, lax.rem(x + t, 4), zl, core), "X", s)

    def w_across(s):
        drain("r", "X", s)
        h = halves[s]
        expect(wg.at[0, :, 0], "S", s)
        send(wg.at[h, :, core], wg.at[h, :, core], sibling, "S", s)

    wg[zh, x, core] = w_ref[rows_half]
    w_along(0)

    def source(r):
        return lax.rem(r // 8, 2) * 32 + lax.rem(r // 4, 2) * 16 + (r // 16) * 4 + lax.rem(r, 4)

    rows64 = lax.broadcasted_iota(jnp.int32, (64, 64), 0)
    cols64 = lax.broadcasted_iota(jnp.int32, (64, 64), 1)
    perm = jnp.where(source(rows64) == cols64, 1.0, 0.0).astype(BF16)
    unperm = jnp.where(source(cols64) == rows64, 1.0, 0.0).astype(BF16)

    def to_plane(src, dst, *key):
        @pl.loop(1, 16)
        def _(t):
            ty, tx = plane(t)
            send(src(ty, tx), dst, dev(zh, ty, tx, zl, core), *key)

    def spread_cotangent(c):
        drain("r", "A", G, c, 0)
        pump()
        own = g_ref[c, :, mine, :].reshape(32, D)
        both = jnp.concatenate([own, gin[c].reshape(32, D)], axis=0)
        xg[c] = dot(perm, both, NN).astype(BF16).reshape(4, 16, D)
        expect(rg.at[c, pl.ds(0, 15)], "B", G, c)
        to_plane(lambda ty, tx: xg.at[c, tx], rg.at[c, me], "B", G, c)
        rg[c, me] = xg[c, x]

    def arranged(a, c, s):
        drain("r", "A", a, c, s)
        pump()
        own = ins[a][c, :, mine, cols(halves[s])].reshape(32, HALF)
        both = jnp.concatenate([own, zin[a, c, s].reshape(32, HALF)], axis=0)
        return dot(perm, both, NN).astype(BF16)

    def spread(c, s):
        for a in (Q, K):
            out = arranged(a, c, s)
            for i in range(4):
                for j in range(4):
                    xqk[c, s, i * 4 + j, a] = out[i * 16:i * 16 + 16, j * 256:j * 256 + 256]
        expect(rqk.at[c, s, pl.ds(0, 15)], "B", Q, c, s)
        to_plane(lambda ty, tx: xqk.at[c, s, tx * 4 + ty], rqk.at[c, s, me], "B", Q, c, s)
        rqk[c, s, me] = xqk[c, s, x * 4 + y]
        out = arranged(V, c, s)
        for i in range(4):
            for j in range(4):
                xv[c, s, i * 4 + j] = out[i * 16:i * 16 + 16, j * 256:j * 256 + 256]
        expect(rv.at[c, s, pl.ds(0, 15)], "B", V, c, s)
        to_plane(lambda ty, tx: xv.at[c, s, tx * 4 + ty], rv.at[c, s, me], "B", V, c, s)
        rv[c, s, me] = xv[c, s, x * 4 + y]

    lane = lax.broadcasted_iota(jnp.int32, (256, 256), 1)
    line = lax.broadcasted_iota(jnp.int32, (256, 256), 0)
    same = lax.rem(lane, 4) == lax.rem(line, 4)

    def attend(c, s):
        drain("r", "S", s)
        drain("r", "B", G, c)
        ga_both = dot(rg[c].reshape(256, D), wg[halves[s]].reshape(256, D), NT).astype(BF16)
        drain("r", "B", Q, c, s)
        drain("r", "B", V, c, s)
        for i in range(2):
            col = slice(i * HEAD_DIM, i * HEAD_DIM + HEAD_DIM)
            query = rqk[c, s, :, 0, :, col].reshape(256, HEAD_DIM)
            key = rqk[c, s, :, 1, :, col].reshape(256, HEAD_DIM)
            value = rv[c, s, :, :, col].reshape(256, HEAD_DIM)
            ga = ga_both[:, col]
            scores = jnp.where(same, dot(query, key, NT) * SCALE, -1e30)
            e = jnp.exp(scores - jnp.max(scores, axis=1, keepdims=True))
            probs = e * (1.0 / jnp.sum(e, axis=1, keepdims=True))
            low = probs.astype(BF16)
            att[c, s, :, col] = dot(low, value, NN).astype(BF16)
            gp = dot(ga, value, NT)
            delta = jnp.sum(probs * gp, axis=1, keepdims=True)
            gs = (probs * (gp - delta)).astype(BF16)
            os[c, s, :, Q, :, col] = (dot(gs, key, NN) * SCALE).astype(BF16).reshape(16, 16, HEAD_DIM)
            os[c, s, :, K, :, col] = (dot(gs, query, TN) * SCALE).astype(BF16).reshape(16, 16, HEAD_DIM)
            os[c, s, :, V, :, col] = dot(low, ga, TN).astype(BF16).reshape(16, 16, HEAD_DIM)
        slot = x * 4 + y
        expect(ro.at[c, s, pl.ds(0, 15)], "R", c, s)
        to_plane(lambda ty, tx: os.at[c, s, ty * 4 + tx], ro.at[c, s, slot], "R", c, s)
        ro[c, s, slot] = os[c, s, me]

    def give_back(c, s):
        drain("r", "R", c, s)
        for a in range(3):
            parts = [
                jnp.concatenate([ro[c, s, i * 4 + j, a] for j in range(4)], axis=1) for i in range(4)
            ]
            out = dot(unperm, jnp.concatenate(parts, axis=0), NN).astype(BF16)
            zs[a, c, s] = out[32:].reshape(2, 16, HALF)
            expect(zs.at[a, c, s], "D", a, c, s)
            send(zs.at[a, c, s], outs[a].at[c, :, mine, cols(halves[s])], pair, "D", a, c, s)
            outs[a][c, :, mine, cols(halves[s])] = out[:32].reshape(2, 16, HALF)

    def weight_first(s):
        for c in range(2):
            att_t[:, c * 256:c * 256 + 256] = att[c, s].T

        @pl.loop(0, 8)
        def _(n):
            col = pl.ds(pl.multiple_of(n * 256, 256), 256)
            part = dot(att_t[...], rg[:, :, :, col].reshape(512, 256), NN)
            part = part.reshape(4, 4, 2, 8, 256)
            for i in range(2):
                g1s[s, i, :, :, col] = part[:, :, i].reshape(4, 32, 256).astype(BF16)

        expect(g1r.at[s], "P", 0, s)
        send(g1s.at[s, 1 - core], g1r.at[s], sibling, "P", 0, s)

    def weight_second(s):
        drain("r", "P", 0, s)
        for i in range(4):
            g2s[s, i] = (g1s[s, core, i].astype(F32) + g1r[s, i].astype(F32)).astype(BF16)
        expect(g2r.at[s, pl.ds(0, 3)], "P", 1, s)

        @pl.loop(1, 4)
        def _(t):
            tx = lax.rem(x + t, 4)
            send(g2s.at[s, tx], g2r.at[s, x], dev(zh, y, tx, zl, core), "P", 1, s)

        g2r[s, x] = g2s[s, x]

    def weight_third(s):
        drain("r", "P", 1, s)
        total = (g2r[s, 0].astype(F32) + g2r[s, 1].astype(F32)) + (g2r[s, 2].astype(F32) + g2r[s, 3].astype(F32))
        total = total.reshape(4, 8, D)
        g3s[s] = jnp.concatenate([total[:, :, :HALF], total[:, :, HALF:]], axis=1).astype(BF16)
        z = zh * 4 + zl
        if s == 0:
            g3r[z] = g3s[s, zl]
        expect(g3r.at[pl.ds(0, 3 + s)], "P", 2, s)

        @pl.loop(1 - s, 4)
        def _(t):
            to = lax.rem(zl + t, 4)
            send(g3s.at[s, to], g3r.at[z], dev(halves[s], y, x, to, core), "P", 2, s)

    def weight_last():
        drain("r", "P", 2, 0)
        drain("r", "P", 2, 1)
        total = g3r[0].astype(F32)
        for i in range(1, 8):
            total = total + g3r[i].astype(F32)
        ow_ref[:, :HALF] = total[:8]
        ow_ref[:, HALF:] = total[8:]

    spread_cotangent(0)
    w_across(0)
    spread(0, 0)
    attend(0, 0)
    w_along(1)
    spread(0, 1)
    give_back(0, 0)
    w_across(1)
    spread_cotangent(1)
    attend(0, 1)
    spread(1, 0)
    give_back(0, 1)
    attend(1, 0)
    weight_first(0)
    spread(1, 1)
    give_back(1, 0)
    weight_second(0)
    attend(1, 1)
    weight_first(1)
    weight_third(0)
    weight_second(1)
    give_back(1, 1)
    weight_third(1)
    weight_last()
    for way, key in list(flight):
        drain(way, *key)


def place(*refs):
    sources, targets, sem = refs[:4], refs[4:8], refs[8]
    copies = [pltpu.make_async_copy(a, b, sem.at[i]) for i, (a, b) in enumerate(zip(sources, targets))]
    for copy in copies:
        copy.start()
    for copy in copies:
        copy.wait()


def on_device(queries, keys_saved, values_saved, grad_output, w_out):
    vmem = pl.BlockSpec(memory_space=pltpu.VMEM)
    dma = pltpu.SemaphoreType.DMA
    whole = jax.ShapeDtypeStruct(queries.shape, BF16)

    def buf(*shape):
        return pltpu.VMEM(shape, BF16)

    shapes = (whole, whole, whole, jax.ShapeDtypeStruct((8, D), F32))
    anywhere = pl.BlockSpec(memory_space=pl.ANY)
    results = pl.pallas_call(
        kernel,
        name="attention_backward",
        out_shape=shapes,
        in_specs=[anywhere] * 5,
        out_specs=(vmem,) * 4,
        scratch_shapes=[
            buf(*queries.shape), buf(*queries.shape), buf(*queries.shape), buf(*queries.shape), buf(*w_out.shape),
            buf(2, 2, 16, D),
            buf(3, 2, 2, 2, 16, HALF),
            buf(2, 4, 16, D),
            buf(2, 2, 16, 2, 16, 256),
            buf(2, 2, 16, 16, 256),
            buf(2, 16, 16, D),
            buf(2, 2, 16, 2, 16, 256),
            buf(2, 2, 16, 16, 256),
            buf(2, 4, 2, 32, D),
            buf(2, 2, 256, 256),
            buf(256, 512),
            buf(2, 2, 16, 3, 16, 256),
            buf(2, 2, 16, 3, 16, 256),
            buf(3, 2, 2, 2, 16, HALF),
            buf(2, 2, 4, 32, D),
            buf(2, 4, 32, D),
            buf(2, 4, 32, D),
            buf(2, 4, 32, D),
            buf(2, 4, 16, HALF),
            buf(8, 16, HALF),
            dma((64,)), dma((64,)), dma((5,)),
        ],
        compiler_params=pltpu.CompilerParams(
            collective_id=0, has_side_effects=True, vmem_limit_bytes=56 * 1024 * 1024
        ),
        cost_estimate=pl.CostEstimate(flops=5 * 10**9, bytes_accessed=4 * 2**20, transcendentals=2**20),
    )(queries, keys_saved, values_saved, grad_output, w_out)
    return pl.pallas_call(
        place,
        name="place_results",
        out_shape=shapes,
        in_specs=[vmem] * 4,
        out_specs=(anywhere,) * 4,
        scratch_shapes=[dma((4,))],
        cost_estimate=pl.CostEstimate(flops=0, bytes_accessed=4 * 2**20, transcendentals=0),
    )(*results)


def solution(mesh):
    split = P("dp", "frame", None, None)
    return jax.shard_map(
        on_device,
        mesh=mesh,
        in_specs=(split, split, split, split, P("frame", None)),
        out_specs=(split, split, split, P(("frame", "dp"), None)),
        check_vma=False,
    )
```

time: 1470 us -> 120 us (0.08)
  waiting for transfers between devices: 1370 us -> 0 us
  Pallas kernels: 0 us -> 119 us
  starting transfers between devices: 46.1 us -> 0 us
  local copies, waits for them, and re-layouts: 20.5 us -> 0 us
  matrix products: 17.7 us -> 0 us
  between operations: 15.7 us -> 0.64 us
    reduce_scatter x1 -> x0, waiting for transfers between devices: 1200 us -> none  [on_device(): lax.psum_scatter(jnp.dot(attended_t, grad_flat, preferred_element_type=jn...]
    pallas_call x0 -> x2, Pallas kernels: none -> 119 us  [the longest x1 117 us: on_device(): pl.pallas_call(kernel, name='attention_backward', out_shape=shapes, in_sp...]
    all_to_all x7 -> x0, waiting for transfers between devices: 89.2 us -> none  [the longest x1 20.6 us: on_device(): lax.all_to_all(values_saved, 'frame', split_axis=2, concat_axis=1, tiled=...]
    all_gather x1 -> x0, waiting for transfers between devices: 74.6 us -> none  [on_device(): lax.all_gather(w_out, 'frame', axis=0, tiled=True)]
    all_to_all x7 -> x0, starting transfers between devices: 45.9 us -> none  [the longest x1 14.5 us: on_device(): lax.all_to_all(queries, 'frame', split_axis=2, concat_axis=1, tiled=True)]
    dot_general x7 -> x0, matrix products: 17.2 us -> none  [the longest x1 8.12 us: on_device(): jnp.dot(attended_t, grad_flat, preferred_element_type=jnp.float32)]
  transfers between devices with their start and end apart: 9 -> 0, of which waited for: 9 -> 0; matrix products, arithmetic and copies ran while one was open for 3% -> 0% of each run, Pallas kernels for 0% -> 0%
where the time goes in v2:
time: 120 us
  Pallas kernels  119 us (99%)
    pallas_call x1, Pallas kernels, on_device(): pl.pallas_call(kernel, name='attention_backward', out_shape=shapes, in_sp...  117 us
    pallas_call x1, Pallas kernels, on_device(): pl.pallas_call(place, name='place_results', out_shape=shapes, in_specs=[v...  2.54 us

profile of v2, /device:TPU:1, one launch (start us, length us, event | category | flops | bytes accessed | tf_op | source)
XLA Modules:
  0.0 119.9 jit_solution(8626930093908525948)
XLA Ops:
  0.6 116.7 %attention_backward.1 = (bf16[2,2,32,2048]{3,2,1,0:T(8,128)(2,1)}, bf16[2,2,32,2048]{3,2,1,0:T(8,128)(2,1)}, bf16[2,2,32,2048]{3,2,1,0:T(8,128)(2,1)}, f32[8,2048]{1,0:T(8,128)}) custom-call(bf16[2,2,32,2048]{3,2,1,0:T(8,128)(2,1)} %q_hbm.1, bf16[2,2,32,2048]{3,2,1,0:T(8,128)(2,1)} %k_hbm.1, bf16[2,2,32,2048]{3,2,1,0:T(8,128)(2,1)} %v_hbm.1, ...), custom_call_target="tpu_custom_call" | custom-call | flops 5000000000 | bytes 4194304 | tf_op jit(solution)/shard_map/attention_backward/pallas_call | solution.py:343
  117.4 2.5 %place_results.1 = (bf16[2,2,32,2048]{3,2,1,0:T(8,128)(2,1)}, bf16[2,2,32,2048]{3,2,1,0:T(8,128)(2,1)}, bf16[2,2,32,2048]{3,2,1,0:T(8,128)(2,1)}, f32[8,2048]{1,0:T(8,128)}) custom-call(bf16[2,2,32,2048]{3,2,1,0:T(8,128)(2,1)} %get-tuple-element.8.refs_0_, bf16[2,2,32,2048]{3,2,1,0:T(8,128)(2,1)} %get-tuple-element.9.refs_1_, ...), custom_call_target="tpu_custom_call" | custom-call | bytes 4194304 | tf_op jit(solution)/shard_map/place_results/pallas_call | solution.py:378

commit v3 on v2

--- a/solution.py
+++ b/solution.py
@@ -120,7 +120,10 @@
             elif item[0] == G:
                 c = item[1]
                 expect(gin.at[c], "A", *item)
-                send(g_ref.at[c, :, other], gin.at[c], pair, "A", *item)
+                for i in range(2):
+                    for h in range(2):
+                        col = slice(h * HALF, h * HALF + HALF)
+                        send(g_ref.at[c, i, other, col], gin.at[c, i, :, col], pair, "A", *item)
             else:
                 a, c, s = item
                 expect(zin.at[a, c, s], "A", *item)
@@ -225,13 +228,14 @@
             os[c, s, :, K, :, col] = (dot(gs, query, TN) * SCALE).astype(BF16).reshape(16, 16, HEAD_DIM)
             os[c, s, :, V, :, col] = dot(low, ga, TN).astype(BF16).reshape(16, 16, HEAD_DIM)
         slot = x * 4 + y
-        expect(ro.at[c, s, pl.ds(0, 15)], "R", c, s)
-        to_plane(lambda ty, tx: os.at[c, s, ty * 4 + tx], ro.at[c, s, slot], "R", c, s)
+        for a in range(3):
+            expect(ro.at[c, s, pl.ds(0, 15), a], "R", c, s, a)
+            to_plane(lambda ty, tx: os.at[c, s, ty * 4 + tx, a], ro.at[c, s, slot, a], "R", c, s, a)
         ro[c, s, slot] = os[c, s, me]
 
     def give_back(c, s):
-        drain("r", "R", c, s)
         for a in range(3):
+            drain("r", "R", c, s, a)
             parts = [
                 jnp.concatenate([ro[c, s, i * 4 + j, a] for j in range(4)], axis=1) for i in range(4)
             ]

time: 120 us -> 119 us (level)
  no operation moved by 1% of the time
where the time goes in v3:
time: 119 us
  Pallas kernels  119 us (100%)
    pallas_call x1, Pallas kernels, on_device(): pl.pallas_call(kernel, name='attention_backward', out_shape=shapes, in_sp...  116 us
    pallas_call x1, Pallas kernels, on_device(): pl.pallas_call(place, name='place_results', out_shape=shapes, in_specs=[v...  2.54 us

profile of v3, /device:TPU:1, one launch (start us, length us, event | category | flops | bytes accessed | tf_op | source)
XLA Modules:
  0.0 119.2 jit_solution(16178910866585777681)
XLA Ops:
  0.6 116.1 %attention_backward.1 = (bf16[2,2,32,2048]{3,2,1,0:T(8,128)(2,1)}, bf16[2,2,32,2048]{3,2,1,0:T(8,128)(2,1)}, bf16[2,2,32,2048]{3,2,1,0:T(8,128)(2,1)}, f32[8,2048]{1,0:T(8,128)}) custom-call(bf16[2,2,32,2048]{3,2,1,0:T(8,128)(2,1)} %q_hbm.1, bf16[2,2,32,2048]{3,2,1,0:T(8,128)(2,1)} %k_hbm.1, bf16[2,2,32,2048]{3,2,1,0:T(8,128)(2,1)} %v_hbm.1, ...), custom_call_target="tpu_custom_call" | custom-call | flops 5000000000 | bytes 4194304 | tf_op jit(solution)/shard_map/attention_backward/pallas_call | solution.py:347
  116.7 2.5 %place_results.1 = (bf16[2,2,32,2048]{3,2,1,0:T(8,128)(2,1)}, bf16[2,2,32,2048]{3,2,1,0:T(8,128)(2,1)}, bf16[2,2,32,2048]{3,2,1,0:T(8,128)(2,1)}, f32[8,2048]{1,0:T(8,128)}) custom-call(bf16[2,2,32,2048]{3,2,1,0:T(8,128)(2,1)} %get-tuple-element.8.refs_0_, bf16[2,2,32,2048]{3,2,1,0:T(8,128)(2,1)} %get-tuple-element.9.refs_1_, ...), custom_call_target="tpu_custom_call" | custom-call | bytes 4194304 | tf_op jit(solution)/shard_map/place_results/pallas_call | solution.py:382

commit v4 on v3

--- a/solution.py
+++ b/solution.py
@@ -36,7 +36,7 @@
     q_hbm, k_hbm, v_hbm, g_hbm, w_hbm,
     oq_ref, ok_ref, ov_ref, ow_ref,
     q_ref, k_ref, v_ref, g_ref, w_ref,
-    gin, zin, xg, xqk, xv, rg, rqk, rv, wg, att, att_t, os, ro, zs, g1s, g1r, g2s, g2r, g3s, g3r,
+    gin, zin, xg, xqk, xv, rg, rqk, rv, wg, att, att_t, os, ro, zs, zo, g1s, g1r, g2s, g2r, g3s, g3r,
     ssem, rsem, lsem,
 ):
     zh, y, x, zl, core = coords()
@@ -233,6 +233,8 @@
             to_plane(lambda ty, tx: os.at[c, s, ty * 4 + tx, a], ro.at[c, s, slot, a], "R", c, s, a)
         ro[c, s, slot] = os[c, s, me]
 
+    keeps = []
+
     def give_back(c, s):
         for a in range(3):
             drain("r", "R", c, s, a)
@@ -243,7 +245,12 @@
             zs[a, c, s] = out[32:].reshape(2, 16, HALF)
             expect(zs.at[a, c, s], "D", a, c, s)
             send(zs.at[a, c, s], outs[a].at[c, :, mine, cols(halves[s])], pair, "D", a, c, s)
-            outs[a][c, :, mine, cols(halves[s])] = out[:32].reshape(2, 16, HALF)
+            zo[a, c, s] = out[:32].reshape(2, 16, HALF)
+            kept = pltpu.make_async_copy(
+                zo.at[a, c, s], outs[a].at[c, :, mine, cols(halves[s])], lsem.at[5 + len(keeps)]
+            )
+            kept.start()
+            keeps.append(kept)
 
     def weight_first(s):
         for c in range(2):
@@ -321,6 +328,8 @@
     give_back(1, 1)
     weight_third(1)
     weight_last()
+    for kept in keeps:
+        kept.wait()
     for way, key in list(flight):
         drain(way, *key)
 
@@ -349,7 +358,7 @@
         name="attention_backward",
         out_shape=shapes,
         in_specs=[anywhere] * 5,
-        out_specs=(vmem,) * 4,
+        out_specs=(anywhere, anywhere, anywhere, vmem),
         scratch_shapes=[
             buf(*queries.shape), buf(*queries.shape), buf(*queries.shape), buf(*queries.shape), buf(*w_out.shape),
             buf(2, 2, 16, D),
@@ -366,13 +375,14 @@
             buf(2, 2, 16, 3, 16, 256),
             buf(2, 2, 16, 3, 16, 256),
             buf(3, 2, 2, 2, 16, HALF),
+            buf(3, 2, 2, 2, 16, HALF),
             buf(2, 2, 4, 32, D),
             buf(2, 4, 32, D),
             buf(2, 4, 32, D),
             buf(2, 4, 32, D),
             buf(2, 4, 16, HALF),
             buf(8, 16, HALF),
-            dma((64,)), dma((64,)), dma((5,)),
+            dma((64,)), dma((64,)), dma((17,)),
         ],
         compiler_params=pltpu.CompilerParams(
             collective_id=0, has_side_effects=True, vmem_limit_bytes=56 * 1024 * 1024

time: 119 us -> 119 us (level)
  no operation moved by 1% of the time
where the time goes in v4:
time: 119 us
  Pallas kernels  118 us (99%)
    pallas_call x1, Pallas kernels, on_device(): pl.pallas_call(kernel, name='attention_backward', out_shape=shapes, in_sp...  116 us
    pallas_call x1, Pallas kernels, on_device(): pl.pallas_call(place, name='place_results', out_shape=shapes, in_specs=[v...  2.54 us

profile of v4, /device:TPU:1, one launch (start us, length us, event | category | flops | bytes accessed | tf_op | source)
XLA Modules:
  0.0 118.9 jit_solution(5274640770592747181)
XLA Ops:
  0.6 115.8 %attention_backward.1 = (bf16[2,2,32,2048]{3,2,1,0:T(8,128)(2,1)}, bf16[2,2,32,2048]{3,2,1,0:T(8,128)(2,1)}, bf16[2,2,32,2048]{3,2,1,0:T(8,128)(2,1)}, f32[8,2048]{1,0:T(8,128)}) custom-call(bf16[2,2,32,2048]{3,2,1,0:T(8,128)(2,1)} %q_hbm.1, bf16[2,2,32,2048]{3,2,1,0:T(8,128)(2,1)} %k_hbm.1, bf16[2,2,32,2048]{3,2,1,0:T(8,128)(2,1)} %v_hbm.1, ...), custom_call_target="tpu_custom_call" | custom-call | flops 5000000000 | bytes 4194304 | tf_op jit(solution)/shard_map/attention_backward/pallas_call | solution.py:356
  116.4 2.5 %place_results.1 = (bf16[2,2,32,2048]{3,2,1,0:T(8,128)(2,1)}, bf16[2,2,32,2048]{3,2,1,0:T(8,128)(2,1)}, bf16[2,2,32,2048]{3,2,1,0:T(8,128)(2,1)}, f32[8,2048]{1,0:T(8,128)}) custom-call(bf16[2,2,32,2048]{3,2,1,0:T(8,128)(2,1)} %get-tuple-element.8.refs_0_, bf16[2,2,32,2048]{3,2,1,0:T(8,128)(2,1)} %get-tuple-element.9.refs_1_, ...), custom_call_target="tpu_custom_call" | custom-call | bytes 4194304 | tf_op jit(solution)/shard_map/place_results/pallas_call | solution.py:392
